TPU v7x, 32 devices: a whole 2x2x4 slice. The times are simulated.
32 devices in a mesh: dp: 8 (over y, x, core), hid: 4 (over z).
Axes of the slice: x: 2, y: 2, z: 4, core: 2. Of those that a mesh axis runs over, the one named last changes fastest.
Arguments:
- tokens: bfloat16 [192, 196, 384], P('dp'), may hold values from -6 to 6
- masks: int32 [192, 196], P('dp'), may hold values 0 or 1
- cotangent: bfloat16 [192, 196, 384], P('dp'), may hold values from -6 to 6
- aff_scale: float32 [2, 2, 384], replicated, may hold values from 0.25 to 1.75
- aff_shift: float32 [2, 2, 384], replicated, may hold values from -3 to 3
- layer_scale: float32 [2, 2, 384], replicated, may hold values from 0.25 to 1.75
- crosspatch_weight: bfloat16 [2, 196, 196], replicated, may hold values from -0.4375 to 0.4375
- cross_bias: float32 [2, 196], replicated, may hold values from -3 to 3
- fc1_weight: bfloat16 [2, 384, 1536], P(None, 'dp', 'hid'), may hold values from -0.3125 to 0.3125
- fc1_bias: float32 [2, 1536], replicated, may hold values from -3 to 3
- fc2_weight: bfloat16 [2, 384, 1536], P(None, 'dp', 'hid'), may hold values from -0.15625 to 0.15625
- fc2_bias: float32 [2, 384], replicated, may hold values from -2 to 2
Outputs:
- output: bfloat16 [192, 196, 384], P('dp')
- tokens_grad: bfloat16 [192, 196, 384], P('dp')
- aff_scale_grad: float32 [2, 2, 384], replicated
- aff_shift_grad: float32 [2, 2, 384], replicated
- layer_scale_grad: float32 [2, 2, 384], replicated
- cross_weight_grad: float32 [2, 196, 196], replicated
- cross_bias_grad: float32 [2, 196], replicated
- fc1_weight_grad: float32 [2, 384, 1536], P(None, 'dp', 'hid')
- fc1_bias_grad: float32 [2, 1536], P(None, 'hid')
- fc2_weight_grad: float32 [2, 384, 1536], P(None, 'dp', 'hid')
- fc2_bias_grad: float32 [2, 384], replicated
All inputs are finite; a program needn't handle non-finite values. No bound on the sum of `masks` on one device may be relied on, other than what follows from the above.
Results may differ from a plain program's by a relative error of at most 0.02.
Values may be sent and summed in bfloat16 or wider, within the bound.
No kernel may reach another device: no remote copies, remote signals or barrier semaphores. Data moves between devices by JAX's collectives and lax.ppermute only.
A program may use at most 256 MiB of HBM per device.

v0:
```python
import jax
import jax.numpy as jnp
from jax import lax
from jax.sharding import PartitionSpec as P


def in_blocks(value, dim, devices):
    before, after = (value.shape[:dim], value.shape[dim + 1 :])
    return jnp.moveaxis(value.reshape(*before, devices, -1, *after), dim, 0)


def summed_on_arrival(value, axis, dim):
    blocks = in_blocks(value, dim, lax.axis_size(axis))
    arrived = lax.all_to_all(blocks, axis, split_axis=0, concat_axis=0, tiled=True)
    return arrived.astype(jnp.float32).sum(axis=0)


def side_by_side(arrays, axis, dim, along):
    both = jnp.concatenate(arrays, axis=along)
    result, at, gathered = (summed_on_arrival(both, axis, dim), 0, [])
    for a in arrays:
        gathered.append(lax.slice_in_dim(result, at, at + a.shape[along], axis=along))
        at += a.shape[along]
    return tuple(gathered)


def gelu_exact(values):
    return jax.nn.gelu(values, approximate=False)


def contract_last(operand, matrix):
    return lax.dot_general(
        operand, matrix, (((1,), (1,)), ((), ())), preferred_element_type=jnp.float32
    )


def contract_rows(operand, matrix):
    return lax.dot_general(
        operand, matrix, (((0,), (0,)), ((), ())), preferred_element_type=jnp.float32
    )


def on_device(
    tokens,
    masks,
    cotangent,
    aff_scale,
    aff_shift,
    layer_scale,
    crosspatch_weight,
    cross_bias,
    fc1_weight,
    fc1_bias,
    fc2_weight,
    fc2_bias,
):
    hid_index = lax.axis_index("hid")
    layer_count = fc1_weight.shape[0]
    hidden_width = fc1_weight.shape[2]
    tokens_here, masks_here, cot_here = (tokens, masks, cotangent)

    def weights_for(current_layer_index):
        weight_pair = (
            lax.all_gather(fc1_weight[current_layer_index], "dp", axis=0, tiled=True),
            lax.all_gather(fc2_weight[current_layer_index], "dp", axis=0, tiled=True),
        )
        return (weight_pair[0], weight_pair[1])

    keep_rows = masks_here.astype(jnp.float32)[:, :, None]
    image_count, patch_count, model_width = tokens_here.shape
    row_count = image_count * patch_count
    stream = tokens_here.astype(jnp.float32)
    saved = []
    for current_layer_index in range(layer_count):
        w_in, w_out = weights_for(current_layer_index)
        mixed_input = (
            (aff_scale[current_layer_index, 0] * stream + aff_shift[current_layer_index, 0])
            * keep_rows
        ).astype(jnp.bfloat16)
        patch_mixed = jnp.einsum(
            "xu,fuo->fxo",
            crosspatch_weight[current_layer_index],
            mixed_input,
            preferred_element_type=jnp.float32,
        )
        patch_mixed = patch_mixed + cross_bias[current_layer_index][None, :, None]
        middle = stream + layer_scale[current_layer_index, 0] * patch_mixed
        normed = (
            (aff_scale[current_layer_index, 1] * middle + aff_shift[current_layer_index, 1])
            .astype(jnp.bfloat16)
            .reshape(row_count, model_width)
        )
        before_activation = jnp.dot(
            normed, w_in, preferred_element_type=jnp.float32
        ) + lax.dynamic_slice_in_dim(
            fc1_bias[current_layer_index], hid_index * hidden_width, hidden_width, 0
        )
        activated = gelu_exact(before_activation).astype(jnp.bfloat16)
        branch_result = lax.psum(
            contract_last(activated, w_out).astype(jnp.bfloat16), "hid"
        ).astype(jnp.float32)
        branch_result = branch_result + fc2_bias[current_layer_index]
        saved.append(
            (
                stream,
                mixed_input,
                patch_mixed,
                middle,
                normed,
                before_activation,
                activated,
                branch_result,
            )
        )
        stream = middle + layer_scale[current_layer_index, 1] * branch_result.reshape(
            image_count, patch_count, model_width
        )
    grad = cot_here.astype(jnp.float32)
    layer_grads = []
    for current_layer_index in reversed(range(layer_count)):
        (
            layer_in,
            mixed_input,
            patch_mixed,
            middle,
            normed,
            before_activation,
            activated,
            branch_result,
        ) = saved[current_layer_index]
        w_in, w_out = weights_for(current_layer_index)
        flat_grad = grad.reshape(row_count, model_width)
        scale_out2 = jnp.sum(flat_grad * branch_result, axis=0)
        branch_grad = (layer_scale[current_layer_index, 1] * flat_grad).astype(jnp.bfloat16)
        bias_out_grad = jnp.sum(branch_grad.astype(jnp.float32), axis=0)
        act_grad = jnp.dot(branch_grad, w_out, preferred_element_type=jnp.float32)
        unused_value, pullback = jax.vjp(gelu_exact, before_activation)
        preact_grad = pullback(act_grad)[0].astype(jnp.bfloat16)
        bias_in_grad = jnp.sum(preact_grad.astype(jnp.float32), axis=0)
        out_weight_grad = contract_rows(branch_grad, activated)
        in_weight_grad = contract_rows(normed, preact_grad)
        normed_grad = lax.psum(contract_last(preact_grad, w_in).astype(jnp.bfloat16), "hid").astype(
            jnp.float32
        )
        middle_flat = middle.reshape(row_count, model_width)
        scale_in2 = jnp.sum(normed_grad * middle_flat, axis=0)
        shift_in2 = jnp.sum(normed_grad, axis=0)
        middle_grad = flat_grad + aff_scale[current_layer_index, 1] * normed_grad
        scale_out1 = jnp.sum(middle_grad * patch_mixed.reshape(row_count, model_width), axis=0)
        crosspatch_gradient = (
            (layer_scale[current_layer_index, 0] * middle_grad)
            .astype(jnp.bfloat16)
            .reshape(image_count, patch_count, model_width)
        )
        cross_bias_grad = jnp.sum(crosspatch_gradient.astype(jnp.float32), axis=(0, 2))
        cross_weight_grad = jnp.einsum(
            "hgi,hvi->gv", crosspatch_gradient, mixed_input, preferred_element_type=jnp.float32
        )
        mixed_grad = (
            jnp.einsum(
                "xa,wxo->wao",
                crosspatch_weight[current_layer_index],
                crosspatch_gradient,
                preferred_element_type=jnp.float32,
            )
            * keep_rows
        )
        scale_in1 = jnp.sum(mixed_grad * layer_in, axis=(0, 1))
        shift_in1 = jnp.sum(mixed_grad, axis=(0, 1))
        grad = (
            middle_grad.reshape(image_count, patch_count, model_width)
            + aff_scale[current_layer_index, 0] * mixed_grad
        )
        weight_grads = (in_weight_grad, out_weight_grad)
        weight_grads = side_by_side(
            (weight_grads[0].astype(jnp.bfloat16), weight_grads[1].astype(jnp.bfloat16)), "dp", 0, 1
        )
        scale_grads = jnp.stack([scale_in1, scale_in2])
        shift_grads = jnp.stack([shift_in1, shift_in2])
        layer_scale_grads = jnp.stack([scale_out1, scale_out2])
        small_sums = lax.psum(
            (
                cross_weight_grad,
                cross_bias_grad,
                scale_grads,
                shift_grads,
                layer_scale_grads,
                bias_out_grad,
                bias_in_grad,
            ),
            "dp",
        )
        bias_in_total = small_sums[6]
        layer_grads.append(
            (
                small_sums[2],
                small_sums[3],
                small_sums[4],
                small_sums[0],
                small_sums[1],
                weight_grads[0],
                bias_in_total,
                weight_grads[1],
                small_sums[5],
            )
        )
    layer_grads = layer_grads[::-1]
    stacked_grads = [jnp.stack([entry[position] for entry in layer_grads]) for position in range(9)]
    result = stream.astype(jnp.bfloat16)
    result_grad = grad.astype(jnp.bfloat16)
    return (
        result,
        result_grad,
        stacked_grads[0],
        stacked_grads[1],
        stacked_grads[2],
        stacked_grads[3],
        stacked_grads[4],
        stacked_grads[5],
        stacked_grads[6],
        stacked_grads[7],
        stacked_grads[8],
    )


def solution(mesh):
    return jax.shard_map(
        on_device,
        mesh=mesh,
        in_specs=(
            P("dp", None, None),
            P("dp", None),
            P("dp", None, None),
            P(),
            P(),
            P(),
            P(),
            P(),
            P(None, "dp", "hid"),
            P(),
            P(None, "dp", "hid"),
            P(),
        ),
        out_specs=(
            P("dp", None, None),
            P("dp", None, None),
            P(),
            P(),
            P(),
            P(),
            P(),
            P(None, "dp", "hid"),
            P(None, "hid"),
            P(None, "dp", "hid"),
            P(),
        ),
        check_vma=False,
    )
```

profile of v0, /device:TPU:0, one launch (start us, length us, event | category | flops | bytes accessed | tf_op | source)
XLA Modules:
  0.0 878.1 jit_solution(15875040874393227630)
XLA Ops:
  14.1 10.9 %all-gather.1 = bf16[1,384,384]{2,1,0:T(8,128)(2,1)S(1)} all-gather(bf16[1,48,384]{2,1,0:T(8,128)(2,1)S(1)} %get-tuple-element.114), channel_id=3, replica_groups=mesh['dp'=8,'hid'=4] {'dp'}, dimensions={1}, use_global_device_ids=true | all-gather | bytes 331776 | tf_op jit(solution)/shard_map/all_gather | solution.py:65
  25.0 9.4 %all-gather = bf16[1,384,384]{2,1,0:T(8,128)(2,1)S(1)} all-gather(bf16[1,48,384]{2,1,0:T(8,128)(2,1)S(1)} %get-tuple-element.116), channel_id=2, replica_groups=mesh['dp'=8,'hid'=4] {'dp'}, dimensions={1}, use_global_device_ids=true | all-gather | bytes 331776 | tf_op jit(solution)/shard_map/all_gather | solution.py:64
  35.8 12.5 %add_convert_fusion.2 = (bf16[24,196,384]{2,1,0:T(8,128)(2,1)}, f32[24,196,384]{2,1,0:T(8,128)}, f32[24,196,384]{2,1,0:T(8,128)}) fusion(f32[384]{0:T(512)S(1)} %get-tuple-element.61, f32[384]{0:T(512)S(1)} %get-tuple-element.57, f32[384]{0:T(512)S(1)} %get-tuple-element.54, bf16[24,196,384]{2,0,1:T(8,128)(2,1)} %param.12, f32[196]{0:T(256)S(1)} %bitcast.126, ...), kind=kOutput, calls=%fused_computation.34 | convolution fusion | flops 729759744 | bytes 21780144 | tf_op jit(solution)/shard_map/xu,fuo->fxo/dot_general | solution.py:80
  48.4 5.7 reshape.95
  54.1 20.5 %multiply_convert_fusion.8 = (bf16[4704,384]{1,0:T(8,128)(2,1)S(1)}, f32[4704,384]{1,0:T(8,128)}, f32[4704,384]{1,0:T(8,128)}) fusion(f32[384]{0:T(512)S(1)} %dynamic-slice_reduce_fusion.1, bf16[4704,384]{1,0:T(8,128)(2,1)} %reshape.95, bf16[1,384,384]{2,1,0:T(8,128)(2,1)S(1)} %all-gather), kind=kOutput, calls=%fused_computation.71 | convolution fusion | flops 1506484224 | bytes 21972480 | tf_op jit(solution)/shard_map/dot_general | solution.py:93
  80.5 5.5 copy_convert_fusion
  86.1 7.8 reshape.99
  94.5 9.4 %all-gather.3 = bf16[1,384,384]{2,1,0:T(8,128)(2,1)} all-gather(bf16[1,48,384]{2,1,0:T(8,128)(2,1)S(1)} %get-tuple-element.113), channel_id=5, replica_groups=mesh['dp'=8,'hid'=4] {'dp'}, dimensions={1}, use_global_device_ids=true | all-gather | bytes 331776 | tf_op jit(solution)/shard_map/all_gather | solution.py:65
  103.9 10.6 %all-gather.2 = bf16[1,384,384]{2,1,0:T(8,128)(2,1)} all-gather(bf16[1,48,384]{2,1,0:T(8,128)(2,1)S(1)} %get-tuple-element.115), channel_id=4, replica_groups=mesh['dp'=8,'hid'=4] {'dp'}, dimensions={1}, use_global_device_ids=true | all-gather | bytes 331776 | tf_op jit(solution)/shard_map/all_gather | solution.py:64
  115.1 102.3 %all-reduce.8.cloned.1.call-done = bf16[4704,384]{1,0:T(8,128)(2,1)} async-done(((bf16[4704,384]{1,0:T(8,128)(2,1)}), bf16[4704,384]{1,0:T(8,128)(2,1)}) %all-reduce.8.cloned.1.call-update) | async-done | bytes 3612688 | tf_op jit(solution)/shard_map/psum | solution.py:99
  217.4 5.4 convert_add_fusion.2
  222.7 7.5 reshape.96
  230.3 5.9 multiply_add_fusion.1
  236.3 8.2 add_convert_fusion.1
  244.7 5.8 reshape.97
  250.6 20.6 %multiply_convert_fusion.7 = (bf16[4704,384]{1,0:T(8,128)(2,1)}, f32[4704,384]{1,0:T(8,128)S(1)}, f32[4704,384]{1,0:T(8,128)}) fusion(f32[384]{0:T(512)} %dynamic-slice_reduce_fusion, bf16[4704,384]{1,0:T(8,128)(2,1)} %reshape.97, bf16[1,384,384]{2,1,0:T(8,128)(2,1)} %all-gather.2), kind=kOutput, calls=%fused_computation.57 | convolution fusion | flops 1506484224 | bytes 21972480 | tf_op jit(solution)/shard_map/dot_general | solution.py:93
  271.2 7.8 convert_reduce_fusion.4
  285.2 7.6 reshape.106
  292.8 6.2 convolution_convert_fusion.2
  299.0 121.5 %all-reduce.10.cloned.1.call-done = bf16[4704,384]{1,0:T(8,128)(2,1)} async-done(((bf16[4704,384]{1,0:T(8,128)(2,1)}), bf16[4704,384]{1,0:T(8,128)(2,1)}) %all-reduce.10.cloned.1.call-update) | async-done | bytes 3612688 | tf_op jit(solution)/shard_map/psum | solution.py:142
  420.6 12.4 %convert_reduce_fusion.1 = (f32[384]{0:T(512)}, f32[384]{0:T(512)}, f32[4704]{0:T(1024)}, bf16[4704,384]{1,0:T(8,128)(2,1)}, f32[4704,384]{1,0:T(8,128)}) fusion(bf16[4704,384]{1,0:T(8,128)(2,1)} %all-reduce.10.cloned.1.call-done, f32[4704,384]{1,0:T(8,128)} %reshape.106, f32[4704,384]{1,0:T(8,128)} %reshape.99, f32[384]{0:T(512)S(1)} %copy-done.22, ...), kind=kLoop, calls=%fused_computation.6 | loop fusion | flops 18057888 | bytes 28926336 | tf_op jit(solution)/shard_map/reduce_sum | solution.py:147
  432.9 5.7 reshape.101
  438.7 7.5 reshape.100
  446.2 9.5 %convert_reduce_fusion.3 = (f32[384]{0:T(512)}, f32[24,196,384]{2,1,0:T(8,128)}, f32[24,384,196]{1,2,0:T(8,128)}) fusion(f32[384]{0:T(512)S(1)} %get-tuple-element.53, f32[24,196,384]{2,1,0:T(8,128)} %reshape.100, f32[24,196]{1,0:T(8,128)S(1)} %convert_element_type.122, f32[384]{0:T(512)S(1)} %copy-done.19, bf16[24,196,384]{2,1,0:T(8,128)(2,1)} %reshape.101, ...), kind=kOutput, calls=%fused_computation.26 | convolution fusion | flops 720727680 | bytes 25388960 | tf_op jit(solution)/shard_map/xa,wxo->wao/dot_general | solution.py:160
  455.7 7.7 reshape.102
  463.5 11.0 %convert_reduce_fusion.5 = (f32[384]{0:T(512)S(1)}, bf16[4704,384]{1,0:T(8,128)(2,1)S(1)}) fusion(f32[4704,384]{1,0:T(8,128)} %get-tuple-element.95, f32[4704,384]{1,0:T(8,128)} %get-tuple-element.124, bf16[1,384,384]{2,1,0:T(8,128)(2,1)S(1)} %copy-done.9, f32[4704,384]{1,0:T(8,128)} %reshape.102, f32[384]{0:T(512)S(1)} %get-tuple-element.53), kind=kOutput, calls=%fused_computation.43 | convolution fusion | flops 1419779712 | bytes 25586688 | tf_op jit(solution)/shard_map/dot_general | solution.py:136
  476.3 4.4 convolution_convert_fusion
  480.9 5.4 convolution_convert_fusion.4
  495.3 7.5 reshape.105
  502.9 7.6 reshape.107
  510.4 7.5 reshape.108
  518.1 6.0 multiply_reduce_fusion.1
  524.3 5.4 convolution_convert_fusion.5
  529.7 5.2 fusion.31
  540.5 6.4 convolution_bitcast_fusion
  551.5 182.1 %all-reduce.14.cloned.1.call-done = (bf16[4704,384]{1,0:T(8,128)(2,1)}, bf16[4704,384]{1,0:T(8,128)(2,1)}) async-done(((bf16[4704,384]{1,0:T(8,128)(2,1)}, bf16[4704,384]{1,0:T(8,128)(2,1)}), (bf16[4704,384]{1,0:T(8,128)(2,1)}, bf16[4704,384]{1,0:T(8,128)(2,1)})) %all-reduce.14.cloned.1.call-update) | async-done | bytes 7225360 | tf_op jit(solution)/shard_map/psum | solution.py:99
  733.7 13.0 %convert_reduce_fusion.7 = (f32[4704]{0:T(1024)S(1)}, bf16[4704,384]{1,0:T(8,128)(2,1)}, f32[4704,384]{1,0:T(8,128)}, f32[384]{0:T(512)S(1)}, f32[384]{0:T(512)S(1)}, /*index=5*/f32[384]{0:T(512)S(1)}) fusion(f32[384]{0:T(512)S(1)} %copy-done.38, f32[4704,384]{1,0:T(8,128)} %reshape.102, bf16[4704,384]{1,0:T(8,128)(2,1)} %get-tuple-element.81, ...), kind=kLoop, calls=%fused_computation.45 | loop fusion | flops 25282848 | bytes 32542080 | tf_op jit(solution)/shard_map/reduce_sum | solution.py:155
  746.7 7.5 reshape.103
  754.2 6.0 multiply_reduce_fusion.3
  760.3 7.3 multiply_reduce_fusion
  767.8 5.7 reshape.104
  773.5 5.4 fusion.33
  778.9 7.5 reshape.98
  786.4 9.7 %convert_reduce_fusion.2 = (f32[384]{0:T(512)S(1)}, bf16[24,196,384]{2,1,0:T(8,128)(2,1)}) fusion(f32[384]{0:T(512)S(1)} %copy-done.17, bf16[24,196,384]{2,0,1:T(8,128)(2,1)} %param.14, f32[24,196,384]{2,1,0:T(8,128)} %get-tuple-element.93, f32[24,196,384]{2,1,0:T(8,128)} %reshape.98), kind=kLoop, calls=%fused_computation.24 | loop fusion | flops 14450304 | bytes 21679104 | tf_op jit(solution)/shard_map/reduce_sum | solution.py:135
  796.1 16.6 %fusion.3 = (f32[384]{0:T(512)S(1)}, f32[384]{0:T(512)S(1)}, bf16[24,196,384]{2,1,0:T(8,128)(2,1)}, f32[24,384,196]{1,2,0:T(8,128)}) fusion(f32[24,196]{1,0:T(8,128)S(1)} %convert_element_type.122, bf16[24,196,384]{2,0,1:T(8,128)(2,1)} %param.12, f32[24,196,384]{2,1,0:T(8,128)} %copy-done, f32[24,384,196]{1,2,0:T(8,128)} %get-tuple-element.127, ...), kind=kOutput, calls=%fused_computation.16 | convolution fusion | flops 726146304 | bytes 39839648 | tf_op jit(solution)/shard_map/xa,wxo->wao/dot_general | solution.py:160
  816.8 24.1 %all-reduce = (f32[1,2,384]{2,1,0:T(2,128)S(1)}, f32[1,2,384]{2,1,0:T(2,128)S(1)}, f32[1,2,384]{2,1,0:T(2,128)S(1)}, f32[1,2,384]{2,1,0:T(2,128)S(1)}, f32[1,2,3...) all-reduce(f32[1,2,384]{2,1,0:T(2,128)S(1)} %maximum_bitcast_fusion, ...), channel_id=1, replica_groups=mesh['dp'=8,'hid'=4] {'dp'}, use_global_device_ids=true, to_apply=%region_9.0 | all-reduce | flops 6536 | bytes 52288 | tf_op jit(solution)/shard_map/psum | solution.py:181
  842.7 4.3 copy.51
  849.9 19.4 %all-reduce.12.cloned.1.call-done = (f32[1,196,196]{2,1,0:T(8,128)}, f32[1,196,196]{2,1,0:T(8,128)}) async-done(((f32[1,196,196]{2,1,0:T(8,128)}, f32[1,196,196]{2,1,0:T(8,128)}), (f32[1,196,196]{2,1,0:T(8,128)}, f32[1,196,196]{2,1,0:T(8,128)})) %all-reduce.12.cloned.1.call-update) | async-done | bytes 307344 | tf_op jit(solution)/shard_map/psum | solution.py:181
  (171 shorter events, 54.3 us)
Async XLA Ops:
  7.2 210.2 %all-reduce.8.cloned.1.call-start = ((), (), s32[]{:S(2)}) async-start(), calls=%async_computation.2 | async-start | bytes 7225344 | tf_op jit(solution)/shard_map/psum | solution.py:99
  8.8 39.6 %copy-start.27 = (f32[384]{0:T(512)}, f32[384]{0:T(512)S(1)}, u32[]{:S(2)}) copy-start(f32[384]{0:T(512)S(1)} %get-tuple-element.58) | copy-start | bytes 4612
  8.8 39.5 %copy-start.35 = (f32[384]{0:T(512)}, f32[384]{0:T(512)S(1)}, u32[]{:S(2)}) copy-start(f32[384]{0:T(512)S(1)} %get-tuple-element.57) | copy-start | bytes 4612
  8.8 227.4 %copy-start.18 = (f32[384]{0:T(512)}, f32[384]{0:T(512)S(1)}, u32[]{:S(2)}) copy-start(f32[384]{0:T(512)S(1)} %get-tuple-element.59) | copy-start | bytes 4612
  8.8 227.4 %copy-start.21 = (f32[384]{0:T(512)}, f32[384]{0:T(512)S(1)}, u32[]{:S(2)}) copy-start(f32[384]{0:T(512)S(1)} %get-tuple-element.56) | copy-start | bytes 4612
  9.6 38.7 %copy-start.40 = (f32[384]{0:T(512)}, f32[384]{0:T(512)S(1)}, u32[]{:S(2)}) copy-start(f32[384]{0:T(512)S(1)} %get-tuple-element.62) | copy-start | bytes 4612
  9.6 226.6 %copy-start.29 = (f32[384]{0:T(512)}, f32[384]{0:T(512)S(1)}, u32[]{:S(2)}) copy-start(f32[384]{0:T(512)S(1)} %get-tuple-element.63) | copy-start | bytes 4612
  11.0 37.3 %copy-start.37 = (f32[384]{0:T(512)}, f32[384]{0:T(512)S(1)}, u32[]{:S(2)}) copy-start(f32[384]{0:T(512)S(1)} %get-tuple-element.54) | copy-start | bytes 4612
  11.0 225.2 %copy-start.23 = (f32[384]{0:T(512)}, f32[384]{0:T(512)S(1)}, u32[]{:S(2)}) copy-start(f32[384]{0:T(512)S(1)} %get-tuple-element.55) | copy-start | bytes 4612
  25.0 49.5 %copy-start.8 = (bf16[1,384,384]{2,1,0:T(8,128)(2,1)}, bf16[1,384,384]{2,1,0:T(8,128)(2,1)S(1)}, u32[]{:S(2)}) copy-start(bf16[1,384,384]{2,1,0:T(8,128)(2,1)S(1)} %all-gather.1) | copy-start | bytes 884740
  35.8 12.5 %copy-start.13 = (bf16[1,196,196]{2,0,1:T(2,128)(2,1)}, bf16[1,196,196]{2,0,1:T(2,128)(2,1)S(1)}, u32[]{:S(2)}) copy-start(bf16[1,196,196]{2,0,1:T(2,128)(2,1)S(1)} %get-tuple-element.108) | copy-start | bytes 230500
  80.5 340.1 %all-reduce.10.cloned.1.call-start = ((), (), s32[]{:S(2)}) async-start(), calls=%async_computation.3 | async-start | bytes 7225344 | tf_op jit(solution)/shard_map/psum | solution.py:142
  86.1 28.4 %copy-start.39 = (f32[2,384]{1,0:T(2,128)S(1)}, f32[2,384]{1,0:T(2,128)}, u32[]{:S(2)}) copy-start(f32[2,384]{1,0:T(2,128)} %param.23) | copy-start | bytes 9220
  115.1 115.2 %copy-start.25 = (f32[384]{0:T(512)}, f32[384]{0:T(512)S(1)}, u32[]{:S(2)}) copy-start(f32[384]{0:T(512)S(1)} %get-tuple-element.65) | copy-start | bytes 4612
  236.2 8.5 copy-start
  244.7 26.4 %slice-start = ((s8[7225344]{0:T(1024)(128)(4,1)}), s8[3031040]{0:T(1024)(128)(4,1)S(1)}, s32[]{:S(2)}) async-start(s8[7225344]{0:T(1024)(128)(4,1)} %bitcast.117), calls=%async_computation.6 | async-start | bytes 6062080
  250.6 20.6 %slice-start.1 = ((s8[7225344]{0:T(1024)(128)(4,1)}), s8[4194304]{0:T(1024)(128)(4,1)S(1)}, s32[]{:S(2)}) async-start(s8[7225344]{0:T(1024)(128)(4,1)} %bitcast.117), calls=%async_computation.7 | async-start | bytes 8388608
  250.6 20.6 %copy-start.10 = (bf16[1,384,384]{2,1,0:T(8,128)(2,1)S(1)}, bf16[1,384,384]{2,1,0:T(8,128)(2,1)}, u32[]{:S(2)}) copy-start(bf16[1,384,384]{2,1,0:T(8,128)(2,1)} %all-gather.3) | copy-start | bytes 884740
  250.6 20.6 %copy-start.16 = (f32[384]{0:T(512)S(1)}, f32[384]{0:T(512)}, u32[]{:S(2)}) copy-start(f32[384]{0:T(512)} %get-tuple-element.52) | copy-start | bytes 4612
  271.2 9.6 %copy-start.12 = (bf16[1,384,384]{2,1,0:T(8,128)(2,1)S(1)}, bf16[1,384,384]{2,1,0:T(8,128)(2,1)}, u32[]{:S(2)}) copy-start(bf16[1,384,384]{2,1,0:T(8,128)(2,1)} %all-gather.2) | copy-start | bytes 884740
  284.9 448.7 %all-reduce.14.cloned.1.call-start = ((), (), s32[]{:S(2)}) async-start(), calls=%async_computation.5 | async-start | bytes 14450688 | tf_op jit(solution)/shard_map/psum | solution.py:99
  285.2 7.6 copy-start.11
  292.8 127.7 %copy-start.22 = (f32[384]{0:T(512)S(1)}, f32[384]{0:T(512)}, u32[]{:S(2)}) copy-start(f32[384]{0:T(512)} %copy-done.21) | copy-start | bytes 4612
  292.8 127.7 %copy-start.24 = (f32[384]{0:T(512)S(1)}, f32[384]{0:T(512)}, u32[]{:S(2)}) copy-start(f32[384]{0:T(512)} %copy-done.23) | copy-start | bytes 4612
  438.7 7.5 copy-start.19
  455.7 7.7 copy-start.9
  480.8 7.6 copy-start.3
  491.7 26.2 %all-to-all-start.1 = ((bf16[8,48,768]{2,1,0:T(8,128)(2,1)}), bf16[8,48,768]{2,1,0:T(8,128)(2,1)S(1)}, u32[]{:S(2)}, u32[]{:S(2)}) async-start(bf16[8,48,768]{2,1,0:T(8,128)(2,1)} %bitcast.30), calls=%async_computation.1 | async-start | bytes 1179648 | tf_op jit(solution)/shard_map/all_to_all | solution.py:14
  510.4 7.5 copy-start.42
  518.0 6.1 copy-start.33
  518.0 6.1 copy-start.32
  518.1 6.1 copy-start.15
  518.1 6.2 copy-start.34
  529.7 10.8 %copy-start.20 = (f32[384]{0:T(512)S(1)}, f32[384]{0:T(512)}, u32[]{:S(2)}) copy-start(f32[384]{0:T(512)} %copy-done.18) | copy-start | bytes 4612
  529.7 10.8 %copy-start.30 = (f32[384]{0:T(512)S(1)}, f32[384]{0:T(512)}, u32[]{:S(2)}) copy-start(f32[384]{0:T(512)} %copy-done.29) | copy-start | bytes 4612
  536.1 14.6 %all-to-all-start = ((bf16[8,48,768]{2,1,0:T(8,128)(2,1)}), bf16[8,48,768]{2,1,0:T(8,128)(2,1)S(1)}, u32[]{:S(2)}, u32[]{:S(2)}) async-start(bf16[8,48,768]{2,1,0:T(8,128)(2,1)} %bitcast.28), calls=%async_computation | async-start | bytes 1179648 | tf_op jit(solution)/shard_map/all_to_all | solution.py:14
  540.3 329.1 %all-reduce.12.cloned.1.call-start = ((), (), s32[]{:S(2)}) async-start(), calls=%async_computation.4 | async-start | bytes 819200 | tf_op jit(solution)/shard_map/psum | solution.py:181
  540.5 193.1 %copy-start.26 = (f32[384]{0:T(512)S(1)}, f32[384]{0:T(512)}, u32[]{:S(2)}) copy-start(f32[384]{0:T(512)} %copy-done.25) | copy-start | bytes 4612
  540.5 193.1 %copy-start.36 = (f32[384]{0:T(512)S(1)}, f32[384]{0:T(512)}, u32[]{:S(2)}) copy-start(f32[384]{0:T(512)} %copy-done.35) | copy-start | bytes 4612
  540.5 193.1 %copy-start.38 = (f32[384]{0:T(512)S(1)}, f32[384]{0:T(512)}, u32[]{:S(2)}) copy-start(f32[384]{0:T(512)} %copy-done.37) | copy-start | bytes 4612
  754.2 6.1 copy-start.7
  754.2 6.1 copy-start.31
  767.6 5.9 copy-start.28
  767.6 5.9 copy-start.41
  786.4 9.7 %copy-start.14 = (bf16[1,196,196]{2,0,1:T(2,128)(2,1)S(1)}, bf16[1,196,196]{2,0,1:T(2,128)(2,1)}, u32[]{:S(2)}) copy-start(bf16[1,196,196]{2,0,1:T(2,128)(2,1)} %copy-done.13) | copy-start | bytes 230500
  786.4 26.4 %slice-start.4 = ((s8[7372800]{0:T(1024)(128)(4,1)}), s8[3178496]{0:T(1024)(128)(4,1)S(1)}, s32[]{:S(2)}) async-start(s8[7372800]{0:T(1024)(128)(4,1)} %bitcast.121), calls=%async_computation.10 | async-start | bytes 6356992
  796.1 16.6 %slice-start.5 = ((s8[7372800]{0:T(1024)(128)(4,1)}), s8[4194304]{0:T(1024)(128)(4,1)S(1)}, s32[]{:S(2)}) async-start(s8[7372800]{0:T(1024)(128)(4,1)} %bitcast.121), calls=%async_computation.11 | async-start | bytes 8388608
  840.9 6.1 copy-start.4
  (7 other events, 27.6 us)
Sparse Core Ops, SparseCore 0:
  80.6 136.7 all-reduce.7
  285.1 135.4 all-reduce.9
  481.0 252.6 all-reduce.13
  816.9 52.4 all-reduce.11
where the time goes:
time: 889 us; the launch traced here: 878 us
  waiting for transfers between devices  429 us (48%)
  matrix products  156 us (18%)
  local copies, waits for them, and re-layouts  126 us (14%)
  other arithmetic  80.4 us (9%)
  blocking collectives  64.4 us (7%)
  between operations  14.6 us (2%)
    psum x2, waiting for transfers between devices, on_device(): lax.psum(contract_last(activated, w_out).astype(jnp.bfloat16), 'hid')  284 us
    psum x1, waiting for transfers between devices, on_device(): lax.psum(contract_last(preact_grad, w_in).astype(jnp.bfloat16), 'hid')  122 us
    dot_general x2, matrix products, on_device(): jnp.dot(normed, w_in, preferred_element_type=jnp.float32)  41.1 us
    dot_general x2, matrix products, on_device(): jnp.einsum('xa,wxo->wao', crosspatch_weight[current_layer_index], crosspa...  26.2 us
    psum x1, blocking collectives, on_device(): lax.psum((cross_weight_grad, cross_bias_grad, scale_grads, shift_grads, l...  24.1 us
    dot_general x2, matrix products, on_device(): jnp.einsum('xu,fuo->fxo', crosspatch_weight[current_layer_index], mixed_i...  20.8 us
    all_gather x2, blocking collectives, weights_for(): lax.all_gather(fc2_weight[current_layer_index], 'dp', axis=0, tiled=True)  20.3 us
    all_gather x2, blocking collectives, weights_for(): lax.all_gather(fc1_weight[current_layer_index], 'dp', axis=0, tiled=True)  20 us
  transfers between devices with their start and end apart: 6, of which 5 were waited for; matrix products, arithmetic and copies ran while one was open for 11% of the time, Pallas kernels for 0%

commit v1 on v0

v1 whole, which is shorter than its diff:
```python
import functools

import jax
import jax.numpy as jnp
from jax import lax
from jax.experimental import pallas as pl
from jax.experimental.pallas import tpu as pltpu
from jax.sharding import PartitionSpec as P

BF = jnp.bfloat16
F32 = jnp.float32
NN = (((1,), (0,)), ((), ()))
NT = (((1,), (1,)), ((), ()))
TN = (((0,), (0,)), ((), ()))
SQRT_HALF = 0.7071067811865476
PDF_SCALE = 0.3989422804014327
S0, T0, S1, T1, LS0, LS1, B2, B1 = range(8)


def dot(a, b, dims):
    return lax.dot_general(a, b, dims, preferred_element_type=F32)


def partial_rows(v):
    return jnp.sum(v.reshape(v.shape[0] // 8, 8, v.shape[1]), axis=0)


def fused_kernel(
    cfg,
    own_ref,
    tok_ref,
    keep_ref,
    cot_ref,
    scale_ref,
    shift_ref,
    ls_ref,
    wc_ref,
    w1_ref,
    b1_ref,
    w2_ref,
    b2_ref,
    out_ref,
    tgrad_ref,
    w1g_ref,
    w2g_ref,
    cwg_ref,
    sums_ref,
    x_s,
    mid_s,
    grad_s,
    mixed_s,
    crossed_s,
    normed_s,
    h_s,
    phi_s,
    act_s,
    branch_s,
    bg_s,
    pg_s,
    cg_s,
):
    layers, patches, rows, images, width, own_width = cfg
    step = pl.program_id(0)
    whole = patches // 16 * 16
    pair = 2 * rows
    blocks = [slice(r, min(r + pair, images * rows)) for r in range(0, images * rows, pair)]

    @pl.when(step == 0)
    def _():
        for ref in (w1g_ref, w2g_ref, cwg_ref, sums_ref, x_s, grad_s):
            ref[...] = jnp.zeros_like(ref)

    own = pl.ds(pl.multiple_of(own_ref[0] * own_width, 128), own_width)
    lane = lax.broadcasted_iota(jnp.int32, (1, rows), 1)

    def row(ref, l, k):
        return ref[l, k : k + 1, :]

    def image(g):
        return slice(g * rows, (g + 1) * rows)

    def add(l, kind, value):
        sums_ref[l, kind] += partial_rows(value)

    def keep_of(g):
        return keep_ref[g]

    for g in range(images):
        x_s[0, g * rows : g * rows + patches, :] = tok_ref[g].astype(F32)
    for l in range(layers):
        for g in range(images):
            at = image(g)
            x = x_s[l, at, :]
            mixed = x * row(scale_ref, l, 0) + row(shift_ref, l, 0)
            mixed_s[l, g * rows : g * rows + whole, :] = mixed[:whole].astype(BF)
            tail = lax.broadcasted_iota(jnp.int32, (rows - whole, 1), 0) + whole
            mixed_s[l, g * rows + whole : (g + 1) * rows, :] = jnp.where(
                tail < patches, mixed[whole:], 1.0
            ).astype(BF)
            wk = wc_ref[l] * jnp.where(lane < patches, keep_of(g), 1.0).astype(BF)
            crossed = dot(wk, mixed_s[l, at, :], NN)
            crossed_s[l, at, :] = crossed.astype(BF)
            middle = x + row(ls_ref, l, 0) * crossed
            mid_s[l, at, :] = middle
            normed_s[l, at, :] = (middle * row(scale_ref, l, 1) + row(shift_ref, l, 1)).astype(BF)
        for at in blocks:
            h = dot(normed_s[l, at, :], w1_ref[l], NN) + b1_ref[l : l + 1, :]
            phi = 0.5 + 0.5 * lax.erf(h * SQRT_HALF)
            act_s[l, at, :] = (h * phi).astype(BF)
            h_s[l, at, :] = h.astype(BF)
            phi_s[l, at, :] = phi.astype(BF)
        for at in blocks:
            branch = dot(act_s[l, at, :], w2_ref[l], NT) + b2_ref[l : l + 1, :]
            branch_s[l, at, :] = branch.astype(BF)
            x_s[l + 1, at, :] = mid_s[l, at, :] + row(ls_ref, l, 1) * branch
    for g in range(images):
        out_ref[g] = x_s[layers, g * rows : g * rows + patches, :].astype(BF)
        grad_s[g * rows : g * rows + patches, :] = cot_ref[g].astype(F32)

    for l in reversed(range(layers)):
        for at in blocks:
            grad = grad_s[at, :]
            add(l, LS1, grad * branch_s[l, at, :].astype(F32))
            bg = row(ls_ref, l, 1) * grad
            add(l, B2, bg)
            bg_s[at, :] = bg.astype(BF)
        for at in blocks:
            act_grad = dot(bg_s[at, :], w2_ref[l], NN)
            h = h_s[l, at, :].astype(F32)
            slope = phi_s[l, at, :].astype(F32) + h * (jnp.exp(h * h * -0.5) * PDF_SCALE)
            pg_s[at, :] = (act_grad * slope).astype(BF)
        add(l, B1, pg_s[:, own].astype(F32))
        w1g_ref[l] += dot(normed_s[l], pg_s[:, own], TN)
        w2g_ref[l] += dot(bg_s[...], act_s[l, :, own], TN)
        for at in blocks:
            normed_grad = dot(pg_s[at, :], w1_ref[l], NT)
            middle = mid_s[l, at, :]
            add(l, S1, normed_grad * middle)
            add(l, T1, normed_grad)
            middle_grad = grad_s[at, :] + row(scale_ref, l, 1) * normed_grad
            add(l, LS0, middle_grad * crossed_s[l, at, :].astype(F32))
            grad_s[at, :] = middle_grad
            cg_s[at, :] = (row(ls_ref, l, 0) * middle_grad).astype(BF)
        for g in range(images):
            at = image(g)
            keep = keep_of(g)
            cg = cg_s[at, :]
            cwg_ref[l] += dot(cg, mixed_s[l, at, :], NT) * jnp.where(lane < patches, keep, 1.0)
            wk = wc_ref[l] * jnp.where(lane < patches, keep, 0.0).astype(BF)
            mixed_grad = dot(wk, cg, TN)
            add(l, S0, mixed_grad * x_s[l, at, :])
            add(l, T0, mixed_grad)
            grad_s[at, :] += row(scale_ref, l, 0) * mixed_grad
    for g in range(images):
        tgrad_ref[g] = grad_s[g * rows : g * rows + patches, :].astype(BF)


def fused(own, tokens, keep, cotangent, scale, shift, ls, wc, w1, b1, w2, b2, images, own_width):
    count, patches, width = tokens.shape
    layers, _, hidden = w1.shape
    rows = (patches + 15) // 16 * 16
    steps = count // images
    m = images * rows
    vmem = pl.BlockSpec(memory_space=pltpu.VMEM)
    per_chunk = pl.BlockSpec((images, patches, width), lambda i: (i, 0, 0))

    def whole_block(shape):
        return pl.BlockSpec(shape, lambda i: (0,) * len(shape))

    wg = (layers, width, own_width)
    cw = (layers, rows, rows)
    sm = (layers, 8, 8, width)
    flops = count * rows * (12 * width * hidden + 6 * rows * width) * layers
    return pl.pallas_call(
        functools.partial(fused_kernel, (layers, patches, rows, images, width, own_width)),
        grid=(steps,),
        in_specs=[
            pl.BlockSpec(memory_space=pltpu.SMEM),
            per_chunk,
            pl.BlockSpec((images, 1, rows), lambda i: (i, 0, 0)),
            per_chunk,
        ]
        + [vmem] * 8,
        out_specs=[
            per_chunk,
            per_chunk,
            whole_block(wg),
            whole_block(wg),
            whole_block(cw),
            whole_block(sm),
        ],
        out_shape=[
            jax.ShapeDtypeStruct(tokens.shape, BF),
            jax.ShapeDtypeStruct(tokens.shape, BF),
            jax.ShapeDtypeStruct(wg, F32),
            jax.ShapeDtypeStruct(wg, F32),
            jax.ShapeDtypeStruct(cw, F32),
            jax.ShapeDtypeStruct(sm, F32),
        ],
        scratch_shapes=[
            pltpu.VMEM((layers + 1, m, width), F32),
            pltpu.VMEM((layers, m, width), F32),
            pltpu.VMEM((m, width), F32),
            pltpu.VMEM((layers, m, width), BF),
            pltpu.VMEM((layers, m, width), BF),
            pltpu.VMEM((layers, m, width), BF),
            pltpu.VMEM((layers, m, hidden), BF),
            pltpu.VMEM((layers, m, hidden), BF),
            pltpu.VMEM((layers, m, hidden), BF),
            pltpu.VMEM((layers, m, width), BF),
            pltpu.VMEM((m, width), BF),
            pltpu.VMEM((m, hidden), BF),
            pltpu.VMEM((m, width), BF),
        ],
        compiler_params=pltpu.CompilerParams(vmem_limit_bytes=60 * 2**20),
        cost_estimate=pl.CostEstimate(
            flops=flops, bytes_accessed=4 * tokens.size * 2, transcendentals=0
        ),
    )(own, tokens, keep, cotangent, scale, shift, ls, wc, w1, b1, w2, b2)


def on_device(
    tokens,
    masks,
    cotangent,
    aff_scale,
    aff_shift,
    layer_scale,
    crosspatch_weight,
    cross_bias,
    fc1_weight,
    fc1_bias,
    fc2_weight,
    fc2_bias,
):
    count, patches, width = tokens.shape
    layers, shard, own_width = fc1_weight.shape
    rows = (patches + 15) // 16 * 16
    n_dp = lax.axis_size("dp")
    own = lax.axis_index("hid").reshape(1)

    def whole(w):
        w = lax.all_gather(w, "hid", axis=2, tiled=True)
        return lax.all_gather(w, "dp", axis=1, tiled=True)

    w1, w2 = whole(fc1_weight), whole(fc2_weight)
    bias_hi = cross_bias.astype(BF)
    bias_lo = (cross_bias - bias_hi.astype(F32)).astype(BF)
    wc = jnp.concatenate([crosspatch_weight, bias_hi[:, :, None], bias_lo[:, :, None]], axis=2)
    wc = jnp.pad(wc, ((0, 0), (0, rows - patches), (0, rows - patches - 2)))
    keep = jnp.pad(masks.astype(F32)[:, None, :], ((0, 0), (0, 0), (0, rows - patches)))

    out, tgrad, w1g, w2g, cwg, sums = fused(
        own,
        tokens,
        keep,
        cotangent,
        aff_scale,
        aff_shift,
        layer_scale,
        wc,
        w1,
        fc1_bias,
        w2,
        fc2_bias,
        4,
        own_width,
    )

    both = jnp.stack([w1g, w2g]).astype(BF).reshape(2, layers, n_dp, shard, own_width)
    both = jnp.moveaxis(both, 2, 0)
    both = lax.all_to_all(both, "dp", split_axis=0, concat_axis=0, tiled=True)
    both = both.astype(F32).sum(axis=0)
    sums = sums.sum(axis=2)
    cwg, sums = lax.psum((cwg, sums), "dp")
    return (
        out,
        tgrad,
        jnp.stack([sums[:, S0], sums[:, S1]], axis=1),
        jnp.stack([sums[:, T0], sums[:, T1]], axis=1),
        jnp.stack([sums[:, LS0], sums[:, LS1]], axis=1),
        cwg[:, :patches, :patches],
        cwg[:, :patches, patches],
        both[0],
        sums[:, B1],
        both[1],
        sums[:, B2],
    )


def solution(mesh):
    return jax.shard_map(
        on_device,
        mesh=mesh,
        in_specs=(
            P("dp", None, None),
            P("dp", None),
            P("dp", None, None),
            P(),
            P(),
            P(),
            P(),
            P(),
            P(None, "dp", "hid"),
            P(),
            P(None, "dp", "hid"),
            P(),
        ),
        out_specs=(
            P("dp", None, None),
            P("dp", None, None),
            P(),
            P(),
            P(),
            P(),
            P(),
            P(None, "dp", "hid"),
            P(None, "hid"),
            P(None, "dp", "hid"),
            P(),
        ),
        check_vma=False,
    )
```

time: 889 us -> 266 us (0.30); the launches traced: 878 us -> 266 us
  waiting for transfers between devices: 429 us -> 53 us
  matrix products: 156 us -> 0 us
  Pallas kernels: 0 us -> 103 us
  local copies, waits for them, and re-layouts: 126 us -> 23.7 us
  other arithmetic: 80.4 us -> 5.79 us
    psum x4 -> x1, waiting for transfers between devices: 425 us -> 19.6 us  [on_device(): cwg, sums = lax.psum((cwg, sums), 'dp')]
    dot_general x18 -> x0, matrix products: 156 us -> none  [the longest x2 41.1 us: on_device(): jnp.dot(normed, w_in, preferred_element_type=jnp.float32)]
    pallas_call x0 -> x1, Pallas kernels: none -> 103 us  [fused(): pl.pallas_call(functools.partial(fused_kernel, (layers, patches, rows, im...]
    reshape x14 -> x0, local copies, waits for them, and re-layouts: 98.7 us -> none  [the longest x2 15.5 us: on_device(): flat_grad = grad.reshape(row_count, model_width)]
    reduce_sum x11 -> x2, other arithmetic: 58.5 us -> 0.21 us  [the longest x1 0.16 us: on_device(): both = both.astype(F32).sum(axis=0)]
    all_gather x0 -> x2, waiting for transfers between devices: none -> 33.4 us  [whole(): return lax.all_gather(w, 'dp', axis=1, tiled=True)]
    add x2 -> x0, other arithmetic: 11.3 us -> none  [the longest x1 5.91 us: on_device(): middle + layer_scale[current_layer_index, 1] * branch_result.reshape(imag...]
    all_gather x4 -> x2, blocking collectives: 40.3 us -> 32.9 us  [whole(): w = lax.all_gather(w, 'hid', axis=2, tiled=True)]
  transfers between devices with their start and end apart: 6 -> 4, of which waited for: 5 -> 3; matrix products, arithmetic and copies ran while one was open for 11% -> 10% of each run, Pallas kernels for 0% -> 0%
where the time goes in v1:
time: 266 us
  Pallas kernels  103 us (39%)
  blocking collectives  62.6 us (24%)
  waiting for transfers between devices  53 us (20%)
  local copies, waits for them, and re-layouts  23.7 us (9%)
  between operations  13.8 us (5%)
  other arithmetic  5.79 us (2%)
  starting transfers between devices  3.69 us (1%)
    pallas_call x1, Pallas kernels, fused(): pl.pallas_call(functools.partial(fused_kernel, (layers, patches, rows, im...  103 us
    all_gather x2, waiting for transfers between devices, whole(): return lax.all_gather(w, 'dp', axis=1, tiled=True)  33.4 us
    all_gather x2, blocking collectives, whole(): w = lax.all_gather(w, 'hid', axis=2, tiled=True)  32.9 us
    psum x1, blocking collectives, on_device(): cwg, sums = lax.psum((cwg, sums), 'dp')  29.7 us
    psum x1, waiting for transfers between devices, on_device(): cwg, sums = lax.psum((cwg, sums), 'dp')  19.6 us
    unnamed x13, local copies, waits for them, and re-layouts  18.5 us
  transfers between devices with their start and end apart: 4, of which 3 were waited for; matrix products, arithmetic and copies ran while one was open for 10% of the time, Pallas kernels for 0%

profile of v1, /device:TPU:0, one launch (start us, length us, event | category | flops | bytes accessed | tf_op | source)
XLA Modules:
  0.0 265.6 jit_solution(16841772932365540673)
XLA Ops:
  7.2 0.0 all-gather.3.cloned.1.call-start
  7.2 17.8 %all_gather.12 = bf16[2,48,1536]{2,1,0:T(8,128)(2,1)} all-gather(bf16[2,48,384]{2,1,0:T(8,128)(2,1)} %param.20), channel_id=1, replica_groups=mesh['dp'=8,'hid'=4] {'hid'}, dimensions={2}, use_global_device_ids=true | all-gather | bytes 368640 | tf_op jit(solution)/shard_map/all_gather | solution.py:243
  25.0 0.0 all-gather.3.cloned.1.call-update
  25.0 0.0 all-gather.5.cloned.1.call-start
  25.1 15.1 %all_gather.14 = bf16[2,48,1536]{2,1,0:T(8,128)(2,1)} all-gather(bf16[2,48,384]{2,1,0:T(8,128)(2,1)} %param.22), channel_id=1, replica_groups=mesh['dp'=8,'hid'=4] {'hid'}, dimensions={2}, use_global_device_ids=true | all-gather | bytes 368640 | tf_op jit(solution)/shard_map/all_gather | solution.py:243
  40.2 0.0 all-gather.5.cloned.1.call-update
  40.2 0.7 convert_element_type.21
  41.0 0.8 convert_bitcast_fusion
  41.7 0.2 copy.55
  41.9 0.2 copy.56
  42.1 1.0 copy.54
  43.1 0.0 copy-start
  43.1 4.8 %copy.57.tok_ref = bf16[24,196,384]{2,1,0:T(8,128)(2,1)} copy(bf16[24,196,384]{2,0,1:T(8,128)(2,1)} %param.12) | data formatting | bytes 7225344 | tf_op args[0]
  47.9 0.0 copy-done
  47.9 2.3 copy.58.cot_ref
  50.2 0.6 pad.8.keep_ref
  50.8 0.8 fusion.8.wc_ref
  51.7 2.4 all-gather.3.cloned.1.call-done.w1_ref
  54.1 30.9 %all-gather.5.cloned.1.call-done.w2_ref = bf16[2,384,1536]{2,1,0:T(8,128)(2,1)} async-done(((bf16[2,48,1536]{2,1,0:T(8,128)(2,1)}), bf16[2,384,1536]{2,1,0:T(8,128)(2,1)}) %all-gather.5.cloned.1.call-update) | async-done | bytes 2359312 | tf_op jit(solution)/shard_map/all_gather | solution.py:244
  85.0 103.0 %shard_map.203 = (bf16[24,196,384]{2,1,0:T(8,128)(2,1)}, bf16[24,196,384]{2,1,0:T(8,128)(2,1)}, f32[2,384,384]{2,1,0:T(8,128)}, f32[2,384,384]{2,1,0:T(8,128)}, ...) custom-call(s32[1]{0:T(128)} %bitcast.own_ref, bf16[24,196,384]{2,1,0:T(8,128)(2,1)} %copy.57.tok_ref, ...), custom_call_target="tpu_custom_call" | custom-call | flops 75450286080 | bytes 14450688 | tf_op jit(solution)/shard_map/pallas_call | solution.py:174
  188.0 0.0 copy-start.1
  188.0 1.4 convert.8
  189.5 0.2 copy-done.1
  189.6 0.1 convert.9
  189.7 1.1 copy_bitcast_fusion
  190.9 3.6 %all-to-all-start = ((bf16[8,2,2,48,384]{4,3,2,1,0:T(8,128)(2,1)}), bf16[8,2,2,48,384]{4,3,2,1,0:T(8,128)(2,1)S(1)}, u32[]{:S(2)}, u32[]{:S(2)}) async-start(bf16[8,2,2,48,384]{4,3,2,1,0:T(8,128)(2,1)} %copy_bitcast_fusion), calls=%async_computation | async-start | bytes 2359296 | tf_op jit(solution)/shard_map/all_to_all | solution.py:272
  194.4 0.0 all-reduce.4.cloned.1.call-start
  194.5 0.0 copy-start.2
  194.5 4.4 %copy.61 = bf16[24,196,384]{2,0,1:T(8,128)(2,1)} copy(bf16[24,196,384]{2,1,0:T(8,128)(2,1)} %get-tuple-element.56) | data formatting | bytes 7225344
  198.8 0.0 all-reduce.4.cloned.1.call-update
  198.9 0.0 copy-done.2
  198.9 0.1 reduce_sum.18
  198.9 29.7 %psum.14 = f32[2,8,384]{2,1,0:T(8,128)S(1)} all-reduce(f32[2,8,384]{2,1,0:T(8,128)S(1)} %reduce_sum.18), channel_id=1, replica_groups=mesh['dp'=8,'hid'=4] {'dp'}, use_global_device_ids=true, to_apply=%region_1.2 | all-reduce | flops 6144 | bytes 49152 | tf_op jit(solution)/shard_map/psum | solution.py:275
  228.7 0.6 stack.24
  229.3 4.3 %copy.62 = bf16[24,196,384]{2,0,1:T(8,128)(2,1)} copy(bf16[24,196,384]{2,1,0:T(8,128)(2,1)} %get-tuple-element.57) | data formatting | bytes 7225344
  233.6 0.6 pad_maximum_fusion.1
  234.2 0.6 copy_bitcast_fusion.1
  234.8 19.6 %all-reduce.4.cloned.1.call-done = f32[2,208,208]{2,1,0:T(8,128)} async-done(((f32[2,208,208]{2,1,0:T(8,128)}), f32[2,208,208]{2,1,0:T(8,128)}) %all-reduce.4.cloned.1.call-update) | async-done | bytes 346128 | tf_op jit(solution)/shard_map/psum | solution.py:275
  254.4 1.0 slice.47
  255.4 1.0 copy.63
  256.4 1.8 slice_reduce_fusion
  258.2 0.0 all-to-all-done
  258.2 0.2 convert_reduce_fusion
  258.3 0.7 slice_bitcast_fusion
  (2 shorter events, 0.0 us)
Async XLA Ops:
  7.2 46.9 %all-gather.3.cloned.1.call-start = ((), (), s32[]{:S(2)}) async-start(), calls=%async_computation.1 | async-start | bytes 2654208 | tf_op jit(solution)/shard_map/all_gather | solution.py:244
  25.0 60.0 %all-gather.5.cloned.1.call-start = ((), (), s32[]{:S(2)}) async-start(), calls=%async_computation.2 | async-start | bytes 2654208 | tf_op jit(solution)/shard_map/all_gather | solution.py:244
  43.1 4.8 %copy-start = (bf16[24,196,384]{2,0,1:T(8,128)(2,1)S(1)}, bf16[24,196,384]{2,0,1:T(8,128)(2,1)}, u32[]{:S(2)}) copy-start(bf16[24,196,384]{2,0,1:T(8,128)(2,1)} %param.14) | copy-start | bytes 10838020
  188.0 1.6 copy-start.1
  190.9 67.3 %all-to-all-start = ((bf16[8,2,2,48,384]{4,3,2,1,0:T(8,128)(2,1)}), bf16[8,2,2,48,384]{4,3,2,1,0:T(8,128)(2,1)S(1)}, u32[]{:S(2)}, u32[]{:S(2)}) async-start(bf16[8,2,2,48,384]{4,3,2,1,0:T(8,128)(2,1)} %copy_bitcast_fusion), calls=%async_computation | async-start | bytes 2359296 | tf_op jit(solution)/shard_map/all_to_all | solution.py:272
  194.4 60.0 %all-reduce.4.cloned.1.call-start = ((), (), s32[]{:S(2)}) async-start(), calls=%async_computation.3 | async-start | bytes 851968 | tf_op jit(solution)/shard_map/psum | solution.py:275
  194.5 4.4 %copy-start.2 = (f32[2,8,8,384]{3,2,1,0:T(8,128)S(1)}, f32[2,8,8,384]{3,2,1,0:T(8,128)}, u32[]{:S(2)}) copy-start(f32[2,8,8,384]{3,2,1,0:T(8,128)} %get-tuple-element.19) | copy-start | bytes 589828
Sparse Core Ops, SparseCore 0:
  25.2 28.8 all-gather.2
  56.0 29.0 all-gather.4
  199.0 55.3 all-reduce.3
